TPU v7x, 512 devices: a whole 4x4x16 slice. The times are simulated.
512 devices in a mesh: section: 64 (over y, z_lo, core), expert: 8 (over x, z_hi).
Axes of the slice: x: 4, y: 4, z: 16 (z_hi: 2, z_lo: 8; z = z_hi * 8 + z_lo), core: 2. Of those that a mesh axis runs over, the one named last changes fastest.
Arguments:
- up_in: bfloat16 [64, 512, 3584], P('section', 'expert'), may hold values from -6 to 6
- down_in: bfloat16 [64, 512, 3584], P('section', 'expert'), may hold values from -6 to 6
- router: float32 [64, 3584], P('section'), may hold values from -0.1875 to 0.1875
- w_gate: bfloat16 [64, 3584, 1024], P('section', None, 'expert'), may hold values from -0.09375 to 0.09375
- w_up: bfloat16 [64, 3584, 1024], P('section', None, 'expert'), may hold values from -0.09375 to 0.09375
- w_down: bfloat16 [64, 1024, 3584], P('section', 'expert'), may hold values from -0.375 to 0.375
- slots_up: int32 [64, 2, 8, 64], P('section', None, 'expert'), may hold values from 0 to 63, each once within a row
- slots_down: int32 [64, 2, 8, 64], P('section', None, 'expert'), may hold values from 0 to 63, each once within a row
Outputs:
- up_out: bfloat16 [64, 512, 3584], P('section', 'expert')
- down_out: bfloat16 [64, 512, 3584], P('section', 'expert')
Inputs may be any that keep to these rules, and one draw needn't show every extreme that they name: `slots_up`: each device's 64 tokens of a micro-batch at a step hold the slots 0 to 63 once each. `slots_down`: each device's 64 tokens of a micro-batch at a step hold the slots 0 to 63 once each.
All inputs are finite; a program needn't handle non-finite values.
Results may differ from a plain program's by a relative error of at most 0.01.
Values may be sent and summed in bfloat16 or wider, within the bound.
A program may use at most 64 MiB of HBM per device.

v0:
```python
import jax
import jax.numpy as jnp
from jax import lax
from jax.sharding import PartitionSpec as P

CAP = 18


def shifted(value, axis, steps):
    count = lax.axis_size(axis)
    initial, last = (max(0, -steps), min(count, count - steps))
    return lax.ppermute(value, axis, [(source, source + steps) for source in range(initial, last)])


def prepare(x, slot_row, router):
    xf = x.astype(jnp.float32)
    normed = xf * lax.rsqrt(jnp.mean(xf * xf, axis=-1, keepdims=True) + 1e-06)
    affinity = jax.nn.sigmoid(jnp.dot(normed, router, precision=lax.Precision.HIGHEST))
    block = (
        jnp.zeros((CAP, x.shape[1]), jnp.bfloat16)
        .at[slot_row]
        .set(normed.astype(jnp.bfloat16), mode="drop")
    )
    return (xf, affinity, block)


def finish(xf, affinity, slot_row, expert_out):
    picked = expert_out[jnp.minimum(slot_row, CAP - 1)]
    taken = jnp.where((slot_row < CAP)[:, None], picked, jnp.float32(0.0))
    return (xf + affinity[:, None] * taken).astype(jnp.bfloat16)


def expert_hidden(piece, w_gate, w_up):
    gate = jnp.dot(piece, w_gate, preferred_element_type=jnp.float32)
    upper = jnp.dot(piece, w_up, preferred_element_type=jnp.float32)
    return (jax.nn.silu(gate) * upper).astype(jnp.bfloat16)


def single_layer(x, slot_row, router, w_gate, w_up, w_down):
    xf, affinity, block = prepare(x, slot_row, router)
    hidden_all = expert_hidden(lax.all_gather(block, "expert", axis=0, tiled=True), w_gate, w_up)
    expert_out = lax.psum_scatter(
        jnp.dot(hidden_all, w_down, preferred_element_type=jnp.float32).astype(jnp.bfloat16),
        "expert",
        scatter_dimension=0,
        tiled=True,
    ).astype(jnp.float32)
    return finish(xf, affinity, slot_row, expert_out)


def both_streams(up_acts, down_acts, step, slots_up, slots_down, router, w_gate, w_up, w_down):
    slot_up_row = slots_up[0, step, 0]
    slot_down_row = slots_down[0, step, 0]
    first = single_layer(up_acts, slot_up_row, router, w_gate, w_up, w_down)
    second = single_layer(down_acts, slot_down_row, router, w_gate, w_up, w_down)
    return (first, second)


def shards(up_in, down_in, router, w_gate, w_up, w_down, slots_up, slots_down):
    router_col = router[0]
    gate_local = w_gate[0]
    up_local = w_up[0]
    down_local = w_down[0]
    mid_up, mid_down = both_streams(
        up_in[0], down_in[0], 0, slots_up, slots_down, router_col, gate_local, up_local, down_local
    )
    moved_up = shifted(mid_up, "section", 1)
    moved_down = shifted(mid_down, "section", -1)
    up_out, down_out = both_streams(
        moved_up, moved_down, 1, slots_up, slots_down, router_col, gate_local, up_local, down_local
    )
    return (up_out[None], down_out[None])


def solution(mesh):
    in_specs = (
        P("section", "expert", None),
        P("section", "expert", None),
        P("section", None),
        P("section", None, "expert"),
        P("section", None, "expert"),
        P("section", "expert", None),
        P("section", None, "expert", None),
        P("section", None, "expert", None),
    )
    out_specs = (P("section", "expert", None), P("section", "expert", None))
    return jax.shard_map(shards, mesh=mesh, in_specs=in_specs, out_specs=out_specs, check_vma=False)
```

profile of v0, /device:TPU:50, one launch (start us, length us, event | category | flops | bytes accessed | tf_op | source)
XLA Modules:
  0.0 1066.3 jit_solution(17320561335605312479)
XLA Ops:
  5.0 131.1 %all-gather.2 = bf16[8,18,3584]{2,1,0:T(8,128)(2,1)S(1)} all-gather(bf16[1,18,3584]{2,1,0:T(8,128)(2,1)S(1)} %bitcast.188), channel_id=1, replica_groups=mesh['section'=64,'expert'=8] {'expert'}, dimensions={0}, use_global_device_ids=true | all-gather | bytes 1161216 | tf_op jit(solution)/shard_map/all_gather | solution.py:41
  139.4 105.7 %all-gather = bf16[8,18,3584]{2,1,0:T(8,128)(2,1)} all-gather(bf16[1,18,3584]{2,1,0:T(8,128)(2,1)S(1)} %bitcast.189), channel_id=1, replica_groups=mesh['section'=64,'expert'=8] {'expert'}, dimensions={0}, use_global_device_ids=true | all-gather | bytes 1161216 | tf_op jit(solution)/shard_map/all_gather | solution.py:41
  245.1 2.3 reshape.343
  250.3 3.0 convolution_convert_fusion.1
  253.3 3.0 convolution_convert_fusion.3
  256.3 232.8 %fusion.129 = (bf16[24,3584]{1,0:T(8,128)(2,1)}, bf16[24,3584]{1,0:T(8,128)(2,1)S(1)}) fusion(bf16[144,3584]{1,0:T(8,128)(2,1)} %convolution_convert_fusion.3, bf16[144,3584]{1,0:T(8,128)(2,1)} %convolution_convert_fusion.1), kind=kCustom, calls=%all-reduce-scatter.5 | all-reduce-scatter fusion | flops 1376257 | bytes 2410496
  489.1 7.7 collective-permute-start.6
  496.9 1.9 collective-permute-start.7
  498.9 2.4 collective-permute-start.2
  506.0 2.2 fusion.21
  508.3 2.5 fusion.29
  516.4 8.2 concatenate.2
  527.4 2.2 fusion.39
  529.6 1.9 collective-permute-start.1
  531.5 8.3 concatenate
  540.8 2.0 gather_fusion
  542.9 2.2 fusion.34
  545.0 2.4 collective-permute-start
  550.5 121.0 %all-gather.3 = bf16[8,18,3584]{2,1,0:T(8,128)(2,1)} all-gather(bf16[1,18,3584]{2,1,0:T(8,128)(2,1)S(1)} %bitcast.190), channel_id=1, replica_groups=mesh['section'=64,'expert'=8] {'expert'}, dimensions={0}, use_global_device_ids=true | all-gather | bytes 1161216 | tf_op jit(solution)/shard_map/all_gather | solution.py:41
  671.5 2.3 reshape.349
  675.4 3.0 convolution_convert_fusion
  680.0 201.1 %all-gather.1 = bf16[8,18,3584]{2,1,0:T(8,128)(2,1)} all-gather(bf16[1,18,3584]{2,1,0:T(8,128)(2,1)S(1)} %bitcast.187), channel_id=1, replica_groups=mesh['section'=64,'expert'=8] {'expert'}, dimensions={0}, use_global_device_ids=true | all-gather | bytes 1161216 | tf_op jit(solution)/shard_map/all_gather | solution.py:41
  881.1 2.3 reshape.345
  885.0 3.0 convolution_convert_fusion.2
  888.0 138.4 %fusion.128 = (bf16[24,3584]{1,0:T(8,128)(2,1)S(1)}, bf16[24,3584]{1,0:T(8,128)(2,1)S(1)}) fusion(bf16[144,3584]{1,0:T(8,128)(2,1)} %convolution_convert_fusion.2, bf16[144,3584]{1,0:T(8,128)(2,1)} %convolution_convert_fusion), kind=kCustom, calls=%all-reduce-scatter.4 | all-reduce-scatter fusion | flops 1376257 | bytes 2410496
  1026.4 13.4 %collective-permute-start.4 = (bf16[24,3584]{1,0:T(8,128)(2,1)S(1)}, bf16[24,3584]{1,0:T(8,128)(2,1)S(1)}, u32[]{:S(2)}, u32[]{:S(2)}) collective-permute-start(bf16[24,3584]{1,0:T(8,128)(2,1)S(1)} %get-tuple-element.4), channel_id=1, source_target_pairs={{0,1},{1,2},{2,3},{3,4},{4,5},{5,6},{6,7},{8,9},{9,10},{10,11},{11... | collective-permute-start | bytes 516104
  1039.8 8.2 collective-permute-start.8
  1048.1 1.9 collective-permute-start.5
  1050.0 1.9 collective-permute-start.9
  1052.0 1.9 fusion.17
  1054.8 2.4 collective-permute-done.5
  1063.1 2.3 fusion.66
  (92 shorter events, 39.6 us)
Async XLA Ops:
  0.6 249.0 %copy-start = (bf16[1,128,3584]{2,1,0:T(8,128)(2,1)S(1)}, bf16[1,128,3584]{2,1,0:T(8,128)(2,1)}, u32[]{:S(2)}) copy-start(bf16[1,128,3584]{2,1,0:T(8,128)(2,1)} %param.13) | copy-start | bytes 2752516
  3.2 1.8 copy-start.14
  136.1 1.1 copy-start.7
  136.1 1.7 copy-start.5
  138.1 1.3 copy-start.17
  245.1 2.3 copy-start.1
  247.4 1.7 copy-start.3
  249.2 1.2 copy-start.2
  256.3 249.7 %copy-start.4 = (bf16[1,64,3584]{2,1,0:T(8,128)(2,1)S(1)}, bf16[1,64,3584]{2,1,0:T(8,128)(2,1)}, u32[]{:S(2)}) copy-start(bf16[1,64,3584]{2,1,0:T(8,128)(2,1)} %param.9) | copy-start | bytes 1376260
  489.1 21.6 %copy-start.8 = (s32[1,2,1,64]{3,2,1,0:T(1,128)S(1)}, s32[1,2,1,64]{3,2,1,0:T(1,128)}, u32[]{:S(2)}) copy-start(s32[1,2,1,64]{3,2,1,0:T(1,128)} %param.14) | copy-start | bytes 1540
  489.1 22.2 %copy-start.12 = (s32[64]{0:T(128)S(1)}, s32[64]{0:T(128)}, u32[]{:S(2)}) copy-start(s32[64]{0:T(128)} %get-tuple-element.13) | copy-start | bytes 772
  489.1 22.8 %copy-start.13 = (s32[64]{0:T(128)S(1)}, s32[64]{0:T(128)}, u32[]{:S(2)}) copy-start(s32[64]{0:T(128)} %get-tuple-element.19) | copy-start | bytes 772
  489.1 23.4 %copy-start.11 = (s32[64]{0:T(128)S(1)}, s32[64]{0:T(128)}, u32[]{:S(2)}) copy-start(s32[64]{0:T(128)} %get-tuple-element.12) | copy-start | bytes 772
  489.1 27.2 %collective-permute-start.6 = (bf16[24,3584]{1,0:T(8,128)(2,1)S(1)}, bf16[24,3584]{1,0:T(8,128)(2,1)}, u32[]{:S(2)}, u32[]{:S(2)}) collective-permute-start(bf16[24,3584]{1,0:T(8,128)(2,1)S(1)} %get-tuple-element.9), channel_id=1, source_target_pairs={{0,1},{1,2},{2,3},{3,4},{4,5},{5,6},{6,7},{8,9},{9,10},{10,11},{11... | collective-permute-start | bytes 516104
  496.9 19.4 %collective-permute-start.7 = (bf16[18,3584]{1,0:T(8,128)(2,1)S(1)}, bf16[18,3584]{1,0:T(8,128)(2,1)}, u32[]{:S(2)}, u32[]{:S(2)}) collective-permute-start(bf16[18,3584]{1,0:T(8,128)(2,1)S(1)} %slice.26), channel_id=1, source_target_pairs={{0,2},{1,3},{2,4},{3,5},{4,6},{5,7},{8,10},{9,11},{10,12},{11,13},... | collective-permute-start | bytes 387080
  498.9 32.6 %collective-permute-start.2 = (bf16[24,3584]{1,0:T(8,128)(2,1)}, bf16[24,3584]{1,0:T(8,128)(2,1)}, u32[]{:S(2)}, u32[]{:S(2)}) collective-permute-start(bf16[24,3584]{1,0:T(8,128)(2,1)} %get-tuple-element.8), channel_id=1, source_target_pairs={{0,1},{1,2},{2,3},{3,4},{4,5},{5,6},{6,7},{8,9},{9,10},{10,11},{11... | collective-permute-start | bytes 516104
  502.9 28.6 %collective-permute-start.3 = (bf16[18,3584]{1,0:T(8,128)(2,1)}, bf16[18,3584]{1,0:T(8,128)(2,1)}, u32[]{:S(2)}, u32[]{:S(2)}) collective-permute-start(bf16[18,3584]{1,0:T(8,128)(2,1)} %slice.24), channel_id=1, source_target_pairs={{0,2},{1,3},{2,4},{3,5},{4,6},{5,7},{8,10},{9,11},{10,12},{11,13},... | collective-permute-start | bytes 387080
  529.6 17.9 %collective-permute-start.1 = (bf16[64,3584]{1,0:T(8,128)(2,1)}, bf16[64,3584]{1,0:T(8,128)(2,1)}, u32[]{:S(2)}, u32[]{:S(2)}) collective-permute-start(bf16[64,3584]{1,0:T(8,128)(2,1)} %fusion.39), channel_id=1, source_target_pairs={{8,0},{16,8},{24,16},{32,24},{40,32},{48,40},{56,48},{64,56},{72,6... | collective-permute-start | bytes 1376264 | tf_op jit(solution)/shard_map/ppermute | solution.py:12
  540.8 2.0 copy-start.6
  545.0 133.3 %collective-permute-start = (bf16[64,3584]{1,0:T(8,128)(2,1)}, bf16[64,3584]{1,0:T(8,128)(2,1)S(1)}, u32[]{:S(2)}, u32[]{:S(2)}) collective-permute-start(bf16[64,3584]{1,0:T(8,128)(2,1)} %fusion.34), channel_id=1, source_target_pairs={{0,8},{8,16},{16,24},{24,32},{32,40},{40,48},{48,56},{56,64},{64,7... | collective-permute-start | bytes 1376264 | tf_op jit(solution)/shard_map/ppermute | solution.py:12
  548.7 125.1 %copy-start.15 = (f32[64]{0:T(128)}, f32[64]{0:T(128)S(1)}, u32[]{:S(2)}) copy-start(f32[64]{0:T(128)S(1)} %add_rsqrt_fusion) | copy-start | bytes 772
  678.6 204.8 %copy-start.18 = (f32[64]{0:T(128)}, f32[64]{0:T(128)S(1)}, u32[]{:S(2)}) copy-start(f32[64]{0:T(128)S(1)} %add_rsqrt_fusion.2) | copy-start | bytes 772
  888.0 164.0 %copy-start.16 = (f32[64]{0:T(128)S(1)}, f32[64]{0:T(128)}, u32[]{:S(2)}) copy-start(f32[64]{0:T(128)} %copy-done.15) | copy-start | bytes 772
  888.0 164.0 %copy-start.20 = (f32[1,3584]{1,0:T(1,128)S(1)}, f32[1,3584]{1,0:T(1,128)}, u32[]{:S(2)}) copy-start(f32[1,3584]{1,0:T(1,128)} %param.10) | copy-start | bytes 43012
  888.0 165.9 %copy-start.19 = (f32[64]{0:T(128)S(1)}, f32[64]{0:T(128)}, u32[]{:S(2)}) copy-start(f32[64]{0:T(128)} %copy-done.18) | copy-start | bytes 772
  1026.4 30.8 %collective-permute-start.4 = (bf16[24,3584]{1,0:T(8,128)(2,1)S(1)}, bf16[24,3584]{1,0:T(8,128)(2,1)S(1)}, u32[]{:S(2)}, u32[]{:S(2)}) collective-permute-start(bf16[24,3584]{1,0:T(8,128)(2,1)S(1)} %get-tuple-element.4), channel_id=1, source_target_pairs={{0,1},{1,2},{2,3},{3,4},{4,5},{5,6},{6,7},{8,9},{9,10},{10,11},{11... | collective-permute-start | bytes 516104
  1039.8 19.2 %collective-permute-start.8 = (bf16[24,3584]{1,0:T(8,128)(2,1)S(1)}, bf16[24,3584]{1,0:T(8,128)(2,1)S(1)}, u32[]{:S(2)}, u32[]{:S(2)}) collective-permute-start(bf16[24,3584]{1,0:T(8,128)(2,1)S(1)} %get-tuple-element.5), channel_id=1, source_target_pairs={{0,1},{1,2},{2,3},{3,4},{4,5},{5,6},{6,7},{8,9},{9,10},{10,11},{11... | collective-permute-start | bytes 516104
  1048.1 9.1 collective-permute-start.5
  1050.0 9.1 collective-permute-start.9
  1061.9 1.2 copy-start.9
  1063.0 2.3 copy-start.10
where the time goes:
time: 1070 us
  blocking collectives  930 us (87%)
  starting transfers between devices  43.7 us (4%)
  local copies, waits for them, and re-layouts  37 us (3%)
  other arithmetic  25.3 us (2%)
  matrix products  25 us (2%)
    all_gather x4, blocking collectives, single_layer(): lax.all_gather(block, 'expert', axis=0, tiled=True)  559 us
    unnamed x2, blocking collectives  371 us
    unnamed x8, starting transfers between devices  39.4 us
    unnamed x55, local copies, waits for them, and re-layouts  30 us
  transfers between devices with their start and end apart: 10, of which 2 were waited for; matrix products, arithmetic and copies ran while one was open for 5% of the time, Pallas kernels for 0%

commit v1 on v0

v1 whole, which is shorter than its diff:
```python
import functools

import jax
import jax.numpy as jnp
from jax import lax
from jax.experimental import pallas as pl
from jax.experimental.pallas import tpu as pltpu
from jax.sharding import PartitionSpec as P

MESH = pl.DeviceIdType.MESH
CAP = 18
MAIN = 16
G = 512
EPS = 1e-06
F32 = jnp.float32
BF16 = jnp.bfloat16


def iota(shape, axis):
    return lax.broadcasted_iota(jnp.int32, shape, axis)


def slot_of_row(row, k):
    tail = row - MAIN - 2 * k
    return jnp.where(
        row < MAIN, row, jnp.where((tail >= 0) & (tail < CAP - MAIN), MAIN + tail, -1)
    )


def dot(a, b):
    return jnp.dot(a, b, preferred_element_type=F32)


def kernel(
    up_ref, dn_ref, router_ref, su_ref, sd_ref, wg_hbm, wu_hbm, wd_hbm,
    uo_ref, do_ref,
    g_ref, p_ref, r0_ref, r1_ref, zs_ref, zr_ref, b2_ref, m1_ref, m2_ref, aff_ref,
    mys_ref, nbs_ref, wgu_ref, wd_ref, chunks, sections,
    w_sem, agz_s, agz_r, agx_s, agx_r, ago_s, ago_r, own_s, own_r,
    rs1_s, rs1_r, rs0_s, rs0_r, rsz_s, rsz_r, m_s, m_r, n_s, n_r,
):
    s = lax.axis_index("section")
    e = lax.axis_index("expert")
    x = e // 2
    h = e % 2
    other = x * 2 + (1 - h)
    width = up_ref.shape[2]
    groups = width // G
    tokens = up_ref.shape[1]
    in_refs = (up_ref, dn_ref)
    out_refs = (uo_ref, do_ref)
    slot_refs = (su_ref, sd_ref)
    cols = [pl.ds(a * G, (b - a) * G) for a, b in chunks]

    def peer(d):
        return lax.rem(x + d, 4)

    def xdev(d):
        return (s, peer(d) * 2 + h)

    zdev = (s, other)
    step_of = (1, -1)
    has_next = (s < sections - 1, s > 0)
    has_prev = (s > 0, s < sections - 1)

    def remote(src, dst, ssem, rsem, device):
        return pltpu.make_async_remote_copy(
            src_ref=src, dst_ref=dst, send_sem=ssem, recv_sem=rsem,
            device_id=device, device_id_type=MESH,
        )

    def agz(p, st, c):
        if p == 0:
            src, device = g_ref.at[p, st, x, :, cols[c]], zdev
        else:
            src, device = b2_ref.at[st, :, cols[c]], (s + step_of[st], other)
        return remote(
            src, g_ref.at[p, st, 4 + x, :, cols[c]],
            agz_s.at[p, st, c], agz_r.at[p, st, c], device,
        )

    def agx(p, st, d, c):
        blk = g_ref.at[p, st, 4 + x, :, cols[c]]
        return remote(blk, blk, agx_s.at[p, st, d - 1, c], agx_r.at[p, st, d - 1, c], xdev(d))

    def ago(p, st, d):
        blk = g_ref.at[p, st, x]
        return remote(blk, blk, ago_s.at[p, st, d - 1], ago_r.at[p, st, d - 1], xdev(d))

    def own(st):
        return remote(
            b2_ref.at[st], g_ref.at[1, st, x], own_s.at[st], own_r.at[st],
            (s + step_of[st], e),
        )

    def rs1(p, st, d, c):
        return remote(
            p_ref.at[p, st, 4 + peer(d), :, cols[c]], r1_ref.at[p, st, d - 1, :, cols[c]],
            rs1_s.at[p, st, d - 1, c], rs1_r.at[p, st, d - 1, c], xdev(d),
        )

    def rs0(p, st, d):
        return remote(
            p_ref.at[p, st, peer(d)], r0_ref.at[p, st, d - 1],
            rs0_s.at[p, st, d - 1], rs0_r.at[p, st, d - 1], xdev(d),
        )

    def rsz(p, st, c):
        return remote(
            zs_ref.at[p, st, :, cols[c]], zr_ref.at[p, st, :, cols[c]],
            rsz_s.at[p, st, c], rsz_r.at[p, st, c], zdev,
        )

    def mid(st):
        return remote(m1_ref.at[st], m2_ref.at[st], m_s.at[st], m_r.at[st], (s + step_of[st], e))

    def nslots(st):
        return remote(
            mys_ref.at[st], nbs_ref.at[st], n_s.at[st], n_r.at[st], (s - step_of[st], e)
        )

    def place(k, q_row, rows):
        pick = (q_row == slot_of_row(iota((2 * MAIN, tokens), 0), k)).astype(F32).astype(BF16)
        return dot(pick, rows)

    def pack(q_row, normed_of, dst):
        tail = jnp.zeros((MAIN, G), F32)
        for k in range(groups):
            placed = place(k, q_row, normed_of(k))
            dst[:, pl.ds(k * G, G)] = placed[:MAIN].astype(BF16)
            tail = tail + placed[MAIN:]
        dst[:, pl.ds(groups * G, G)] = tail.astype(BF16)

    def stats(load):
        ss = jnp.zeros((tokens, G), F32)
        xr = jnp.zeros((tokens, G), F32)
        for k in range(groups):
            v = load(k)
            ss = ss + v * v
            xr = xr + v * router_ref[:, pl.ds(k * G, G)]
        scale = lax.rsqrt(jnp.sum(ss, axis=1, keepdims=True) / width + EPS)
        affinity = jax.nn.sigmoid(scale * jnp.sum(xr, axis=1, keepdims=True))
        return scale, affinity

    def first(st):
        def load(k):
            return in_refs[st][0, :, pl.ds(k * G, G)].astype(F32)

        scale, affinity = stats(load)
        aff_ref[0, st] = jnp.broadcast_to(affinity, (tokens, 128))
        pack(
            slot_refs[st][0, 0], lambda k: (load(k) * scale).astype(BF16), g_ref.at[0, st, x]
        )

    def gate_up(p, st):
        blocks = 8 * MAIN
        tails = g_ref[p, st, :, :, pl.ds(groups * G, G)].reshape(blocks, G)
        r, c = iota((groups * MAIN, blocks), 0), iota((groups * MAIN, blocks), 1)
        sel = c == 16 * ((r >> 1) & 7) + 2 * (r >> 4) + (r & 1)
        tails = dot(sel.astype(F32).astype(BF16), tails).astype(BF16)
        acc = jnp.zeros((blocks + MAIN, wgu_ref.shape[1]), F32)
        for k in range(groups):
            rows = g_ref[p, st, :, :, pl.ds(k * G, G)].reshape(blocks, G)
            rows = jnp.concatenate([rows, tails[k * MAIN : (k + 1) * MAIN]], axis=0)
            acc = acc + dot(rows, wgu_ref[pl.ds(k * G, G), :])
        half = wgu_ref.shape[1] // 2
        gate, upper = acc[:, :half], acc[:, half:]
        return (gate * jax.nn.sigmoid(gate) * upper).astype(BF16)

    def down(p, st, hidden, tails, c):
        blocks = 8 * MAIN
        for k in range(*chunks[c]):
            if k < groups:
                out = dot(hidden, wd_ref[:, pl.ds(k * G, G)]).astype(BF16)
                p_ref[p, st, :, :, pl.ds(k * G, G)] = out[:blocks].reshape(8, MAIN, G)
                tails.append(out[blocks:])
            else:
                r, q = iota((blocks, groups * MAIN), 1), iota((blocks, groups * MAIN), 0)
                sel = q == 16 * ((r >> 1) & 7) + 2 * (r >> 4) + (r & 1)
                out = dot(sel.astype(F32).astype(BF16), jnp.concatenate(tails, axis=0))
                p_ref[p, st, :, :, pl.ds(groups * G, G)] = out.astype(BF16).reshape(8, MAIN, G)
        for d in (2, 1, 3):
            rs1(p, st, d, c).start()

    def reduce_other(p, st, c):
        for d in (1, 2, 3):
            rs1(p, st, d, c).wait_recv()
        total = p_ref[p, st, 4 + x, :, cols[c]].astype(F32)
        for d in (1, 2, 3):
            total = total + r1_ref[p, st, d - 1, :, cols[c]].astype(F32)
        zs_ref[p, st, :, cols[c]] = total.astype(BF16)
        rsz(p, st, c).start()

    def finish(p, st, load, store):
        for d in (1, 2, 3):
            rs0(p, st, d).wait_recv()
        for c in range(len(chunks)):
            rsz(p, st, c).wait_recv()

        def total(k):
            at = pl.ds(k * G, G)
            v = p_ref[p, st, x, :, at].astype(F32) + zr_ref[p, st, :, at].astype(F32)
            for d in (1, 2, 3):
                v = v + r0_ref[p, st, d - 1, :, at].astype(F32)
            high = v.astype(BF16)
            return high, (v - high.astype(F32)).astype(BF16)

        q_row = slot_refs[st][0, p].astype(F32)
        eye = iota((tokens, tokens), 0) == iota((tokens, tokens), 1)
        q_col = jnp.sum(jnp.where(eye, q_row, 0.0), axis=1, keepdims=True)
        affinity = aff_ref[p, st, :, 0:1]
        tail_high, tail_low = total(groups)
        for k in range(groups):
            high, low = total(k)
            lane = iota((tokens, 4 * MAIN), 1) & (2 * MAIN - 1)
            pick = (q_col == slot_of_row(lane, k).astype(F32)).astype(F32).astype(BF16)
            taken = dot(pick, jnp.concatenate([high, tail_high, low, tail_low], axis=0))
            store(k, (load(k) + affinity * taken).astype(BF16))

    def finish_first(st):
        squares = [jnp.zeros((tokens, G), F32)]

        def load(k):
            return in_refs[st][0, :, pl.ds(k * G, G)].astype(F32)

        def store(k, value):
            m1_ref[st, :, pl.ds(k * G, G)] = value
            value = value.astype(F32)
            squares[0] = squares[0] + value * value

        finish(0, st, load, store)
        scale = lax.rsqrt(jnp.sum(squares[0], axis=1, keepdims=True) / width + EPS)

        @pl.when(has_next[st])
        def _():
            nslots(st).wait_recv()

        def normed(k):
            return (m1_ref[st, :, pl.ds(k * G, G)].astype(F32) * scale).astype(BF16)

        pack(nbs_ref[st, 0:1, 0:tokens], normed, b2_ref.at[st])

        @pl.when(has_next[st])
        def _():
            for c in range(len(chunks)):
                agz(1, st, c).start()
            own(st).start()
            mid(st).start()

    def arrive_own(st):
        @pl.when(has_prev[st])
        def _():
            own(st).wait_recv()

        for d in (2, 1, 3):
            ago(1, st, d).start()

    def relay(p, st, c):
        if p == 0:
            agz(p, st, c).wait_recv()
        else:
            @pl.when(has_prev[st])
            def _():
                agz(p, st, c).wait_recv()
        for d in (2, 1, 3):
            agx(p, st, d, c).start()

    def gathered(p, st):
        for d in (1, 2, 3):
            ago(p, st, d).wait_recv()
            for c in range(len(chunks)):
                agx(p, st, d, c).wait_recv()

    def middle(st):
        @pl.when(has_prev[st])
        def _():
            mid(st).wait_recv()

        _, affinity = stats(lambda k: m2_ref[st, :, pl.ds(k * G, G)].astype(F32))
        aff_ref[1, st] = jnp.broadcast_to(affinity, (tokens, 128))

    def finish_second(st):
        def load(k):
            return m2_ref[st, :, pl.ds(k * G, G)].astype(F32)

        def store(k, value):
            out_refs[st][0, :, pl.ds(k * G, G)] = value

        finish(1, st, load, store)

    def sent_gather(p, st):
        def late():
            for c in range(len(chunks)):
                agz(p, st, c).wait_send()
            if p == 1:
                own(st).wait_send()
                mid(st).wait_send()

        if p == 0:
            late()
        else:
            pl.when(has_next[st])(late)
        for d in (1, 2, 3):
            ago(p, st, d).wait_send()
            for c in range(len(chunks)):
                agx(p, st, d, c).wait_send()

    def sent_reduce(p, st):
        for d in (1, 2, 3):
            rs0(p, st, d).wait_send()
            for c in range(len(chunks)):
                rs1(p, st, d, c).wait_send()
        for c in range(len(chunks)):
            rsz(p, st, c).wait_send()

    half = wg_hbm.shape[2]
    weights = [
        pltpu.make_async_copy(wg_hbm.at[0], wgu_ref.at[:, pl.ds(0, half)], w_sem.at[0]),
        pltpu.make_async_copy(wu_hbm.at[0], wgu_ref.at[:, pl.ds(half, half)], w_sem.at[1]),
        pltpu.make_async_copy(wd_hbm.at[0], wd_ref, w_sem.at[2]),
    ]
    for w in weights:
        w.start()

    barrier = pltpu.get_barrier_semaphore()

    def greet(device):
        pl.semaphore_signal(barrier, inc=1, device_id=device, device_id_type=MESH)

    greet(zdev)
    for d in (1, 2, 3):
        greet(xdev(d))
    for step in (1, -1):
        @pl.when((s + step >= 0) & (s + step < sections))
        def _(step=step):
            greet((s + step, e))
            greet((s + step, other))

    first(0)
    for st in (0, 1):
        mys_ref[st] = jnp.zeros(mys_ref.shape[1:], jnp.int32)
        mys_ref[st, 0:1, 0:tokens] = slot_refs[st][0, 1]

        @pl.when(jnp.logical_not(has_next[st]))
        def _(st=st):
            nbs_ref[st] = jnp.zeros(nbs_ref.shape[1:], jnp.int32)

        @pl.when(jnp.logical_not(has_prev[st]))
        def _(st=st):
            g_ref[1, st, x] = jnp.zeros(g_ref.shape[3:], BF16)
            g_ref[1, st, 4 + x] = jnp.zeros(g_ref.shape[3:], BF16)
            m2_ref[st] = jnp.zeros(m2_ref.shape[1:], BF16)

    neighbours = 4 + 2 * (s > 0).astype(jnp.int32) + 2 * (s < sections - 1).astype(jnp.int32)
    pl.semaphore_wait(barrier, neighbours)

    def send_first(st):
        for c in range(len(chunks)):
            agz(0, st, c).start()
        for d in (2, 1, 3):
            ago(0, st, d).start()

    send_first(0)
    first(1)
    send_first(1)
    for st in (0, 1):
        @pl.when(has_prev[st])
        def _(st=st):
            nslots(st).start()

    n = len(chunks)
    for p in (0, 1):
        for c in range(n):
            relay(p, 0, c)
        if p == 0:
            for w in weights:
                w.wait()
        gathered(p, 0)
        hidden = gate_up(p, 0)
        tails = []
        for c in range(n):
            down(p, 0, hidden, tails, c)
        for d in (2, 1, 3):
            rs0(p, 0, d).start()
        if p == 1:
            arrive_own(1)
        relay(p, 1, 0)
        relay(p, 1, 1)
        reduce_other(p, 0, 0)
        reduce_other(p, 0, 1)
        relay(p, 1, 2)
        reduce_other(p, 0, 2)
        relay(p, 1, 3)
        reduce_other(p, 0, 3)
        gathered(p, 1)
        hidden = gate_up(p, 1)
        tails = []
        for c in range(n):
            down(p, 1, hidden, tails, c)
        for d in (2, 1, 3):
            rs0(p, 1, d).start()
        for c in range(n):
            reduce_other(p, 1, c)
        if p == 0:
            finish_first(0)
            for st in (0, 1):
                sent_gather(0, st)
                sent_reduce(0, st)
                pl.when(has_prev[st])(lambda st=st: nslots(st).wait_send())
            finish_first(1)
            arrive_own(0)
            middle(0)
        else:
            middle(1)
            for st in (0, 1):
                sent_gather(1, st)
            finish_second(0)
            sent_reduce(1, 0)
            finish_second(1)
            sent_reduce(1, 1)


def shards(up_in, down_in, router, w_gate, w_up, w_down, slots_up, slots_down, *, sections):
    _, tokens, width = up_in.shape
    groups = width // G
    packed = width + G
    ends = [(groups + 1) * i // 4 for i in range(5)]
    chunks = list(zip(ends[:-1], ends[1:]))
    n = len(chunks)
    ffd = w_gate.shape[2]
    vmem = pl.BlockSpec(memory_space=pltpu.VMEM)
    hbm = pl.BlockSpec(memory_space=pl.ANY)
    dma = pltpu.SemaphoreType.DMA
    out = jax.ShapeDtypeStruct(up_in.shape, BF16)
    return pl.pallas_call(
        functools.partial(kernel_entry, chunks=chunks, sections=sections),
        name="relay_layers",
        out_shape=(out, out),
        in_specs=[vmem] * 5 + [hbm] * 3,
        out_specs=(vmem, vmem),
        scratch_shapes=[
            pltpu.VMEM((2, 2, 8, MAIN, packed), BF16),
            pltpu.VMEM((2, 2, 8, MAIN, packed), BF16),
            pltpu.VMEM((2, 2, 3, MAIN, packed), BF16),
            pltpu.VMEM((2, 2, 3, MAIN, packed), BF16),
            pltpu.VMEM((2, 2, MAIN, packed), BF16),
            pltpu.VMEM((2, 2, MAIN, packed), BF16),
            pltpu.VMEM((2, MAIN, packed), BF16),
            pltpu.VMEM((2, tokens, width), BF16),
            pltpu.VMEM((2, tokens, width), BF16),
            pltpu.VMEM((2, 2, tokens, 128), F32),
            pltpu.VMEM((2, 8, 128), jnp.int32),
            pltpu.VMEM((2, 8, 128), jnp.int32),
            pltpu.VMEM((width, 2 * ffd), BF16),
            pltpu.VMEM((ffd, width), BF16),
            dma((3,)),
            dma((2, 2, n)), dma((2, 2, n)),
            dma((2, 2, 3, n)), dma((2, 2, 3, n)),
            dma((2, 2, 3)), dma((2, 2, 3)),
            dma((2,)), dma((2,)),
            dma((2, 2, 3, n)), dma((2, 2, 3, n)),
            dma((2, 2, 3)), dma((2, 2, 3)),
            dma((2, 2, n)), dma((2, 2, n)),
            dma((2,)), dma((2,)),
            dma((2,)), dma((2,)),
        ],
        compiler_params=pltpu.CompilerParams(
            collective_id=0, has_side_effects=True, vmem_limit_bytes=48 * 1024 * 1024
        ),
    )(up_in, down_in, router, slots_up, slots_down, w_gate, w_up, w_down)


def kernel_entry(*refs, chunks, sections):
    kernel(*refs[:24], chunks, sections, *refs[24:])


def solution(mesh):
    in_specs = (
        P("section", "expert", None),
        P("section", "expert", None),
        P("section", None),
        P("section", None, "expert"),
        P("section", None, "expert"),
        P("section", "expert", None),
        P("section", None, "expert", None),
        P("section", None, "expert", None),
    )
    out_specs = (P("section", "expert", None), P("section", "expert", None))
    body = functools.partial(shards, sections=mesh.shape["section"])
    return jax.shard_map(body, mesh=mesh, in_specs=in_specs, out_specs=out_specs, check_vma=False)
```

time: 1070 us -> 160 us (0.15)
  the two profiles are of different devices: /device:TPU:50 before, /device:TPU:8 now
where the time goes in v1:
time: 160 us
  Pallas kernels  150 us (94%)
  local copies, waits for them, and re-layouts  9.17 us (6%)
    pallas_call x1, Pallas kernels, shards(): pl.pallas_call(functools.partial(kernel_entry, chunks=chunks, sections=se...  150 us
    unnamed x18, local copies, waits for them, and re-layouts  9.17 us

profile of v1, /device:TPU:8, one launch (start us, length us, event | category | flops | bytes accessed | tf_op | source)
XLA Modules:
  0.0 160.0 jit_solution(3060617933236034302)
XLA Ops:
  0.6 0.0 copy-start
  0.6 1.2 copy-done
  1.8 0.0 copy-start.1
  1.8 1.2 copy-done.1
  3.0 0.0 copy-start.2
  3.0 1.2 copy-done.2
  4.2 0.0 copy-start.3
  4.2 1.0 copy-done.3
  5.2 0.0 copy-start.4
  5.2 1.0 copy-done.4
  6.2 0.0 copy-start.5
  6.2 0.7 copy-done.5
  6.9 0.0 copy-start.6
  6.9 0.7 copy-done.6
  7.6 0.0 copy-start.7
  7.6 0.7 copy-done.7
  8.3 150.2 %relay_layers.1 = (bf16[1,64,3584]{2,1,0:T(8,128)(2,1)S(1)}, bf16[1,64,3584]{2,1,0:T(8,128)(2,1)S(1)}) custom-call(bf16[1,64,3584]{2,1,0:T(8,128)(2,1)S(1)} %copy-done.3, bf16[1,64,3584]{2,1,0:T(8,128)(2,1)S(1)} %copy-done.4, f32[1,3584]{1,0:T(1,128)S(1)} %copy-done.5, s32[1,2,1,64]{3,2,1,0:T(1,128)S(1)} %copy-done.6, s32[1,2,1,64]{3,2,1,0:T(1,128)S(1)} %copy-done.7, ...), custom_call_target="tpu_custom_call" | custom-call | tf_op jit(solution)/shard_map/relay_layers/pallas_call | solution.py:435
  158.5 0.8 copy.12
  159.3 0.8 copy.13
Async XLA Ops:
  0.6 1.2 copy-start
  1.8 1.2 copy-start.1
  3.0 1.2 copy-start.2
  4.2 1.0 copy-start.3
  5.2 1.0 copy-start.4
  6.2 0.7 copy-start.5
  6.9 0.7 copy-start.6
  7.6 0.7 copy-start.7

commit v2 on v1

--- a/solution.py
+++ b/solution.py
@@ -16,6 +16,75 @@
 BF16 = jnp.bfloat16
 
 
+VMEM_LIMIT = 62 * 1024 * 1024
+CHUNKS = 4
+ORDER = [
+    ("begin", 0),
+    ("send_own", 0, 0),
+    ("begin", 1),
+    ("slots",),
+    ("send_own", 0, 1),
+    ("send_shift", 0),
+    ("send_shift", 1),
+    ("relay", 0, 0, 0),
+    ("relay", 0, 0, 1),
+    ("relay", 0, 0, 2),
+    ("relay", 0, 0, 3),
+    ("weights",),
+    ("relay", 0, 1, 0),
+    ("compute", 0, 0),
+    ("relay", 0, 1, 1),
+    ("reduce", 0, 0, 0),
+    ("relay", 0, 1, 3),
+    ("reduce", 0, 0, 1),
+    ("relay", 0, 1, 2),
+    ("reduce", 0, 0, 3),
+    ("send_rows", 0, 0),
+    ("reduce", 0, 0, 2),
+    ("compute", 0, 1),
+    ("send_rows", 0, 1),
+    ("reduce", 0, 1, 1),
+    ("reduce", 0, 1, 2),
+    ("reduce", 0, 1, 3),
+    ("reduce", 0, 1, 0),
+    ("finish_first", 0),
+    ("own", 0),
+    ("finish_first", 1),
+    ("relay", 1, 0, 0),
+    ("relay", 1, 0, 1),
+    ("relay", 1, 0, 2),
+    ("own", 1),
+    ("relay", 1, 0, 3),
+    ("relay", 1, 1, 0),
+    ("relay", 1, 1, 1),
+    ("compute", 1, 0),
+    ("reduce", 1, 0, 0),
+    ("relay", 1, 1, 3),
+    ("reduce", 1, 0, 2),
+    ("reduce", 1, 0, 1),
+    ("relay", 1, 1, 2),
+    ("compute", 1, 1),
+    ("slots_sent",),
+    ("sent_gather", 0, 0),
+    ("sent_gather", 0, 1),
+    ("send_rows", 1, 1),
+    ("reduce", 1, 0, 3),
+    ("reduce", 1, 1, 0),
+    ("reduce", 1, 1, 1),
+    ("reduce", 1, 1, 2),
+    ("reduce", 1, 1, 3),
+    ("send_rows", 1, 0),
+    ("sent_reduce", 0, 0),
+    ("sent_reduce", 0, 1),
+    ("sent_gather", 1, 0),
+    ("sent_gather", 1, 1),
+    ("finish_second", 0),
+    ("finish_second", 1),
+    ("sent_reduce", 1, 0),
+    ("sent_reduce", 1, 1),
+]
+
+
 def iota(shape, axis):
     return lax.broadcasted_iota(jnp.int32, shape, axis)
 
@@ -32,24 +101,24 @@
 
 
 def kernel(
-    up_ref, dn_ref, router_ref, su_ref, sd_ref, wg_hbm, wu_hbm, wd_hbm,
+    up_hbm, dn_hbm, router_hbm, su_hbm, sd_hbm, wg_hbm, wu_hbm, wd_hbm,
     uo_ref, do_ref,
-    g_ref, p_ref, r0_ref, r1_ref, zs_ref, zr_ref, b2_ref, m1_ref, m2_ref, aff_ref,
-    mys_ref, nbs_ref, wgu_ref, wd_ref, chunks, sections,
+    x_ref, router_ref, slots_ref,
+    g_ref, p_ref, r0_ref, r1_ref, zs_ref, zr_ref, b2_ref, m1_ref, m2_ref, dl_ref, dr_ref,
+    aff_ref, mys_ref, nbs_ref, prs_ref, wgu_ref, wd_ref, chunks, sections,
     w_sem, agz_s, agz_r, agx_s, agx_r, ago_s, ago_r, own_s, own_r,
-    rs1_s, rs1_r, rs0_s, rs0_r, rsz_s, rsz_r, m_s, m_r, n_s, n_r,
+    rs1_s, rs1_r, rs0_s, rs0_r, rsz_s, rsz_r, m_s, m_r, n_s, n_r, o_s, o_r,
 ):
     s = lax.axis_index("section")
     e = lax.axis_index("expert")
     x = e // 2
     h = e % 2
     other = x * 2 + (1 - h)
-    width = up_ref.shape[2]
+    width = x_ref.shape[2]
     groups = width // G
-    tokens = up_ref.shape[1]
-    in_refs = (up_ref, dn_ref)
+    tokens = x_ref.shape[1]
     out_refs = (uo_ref, do_ref)
-    slot_refs = (su_ref, sd_ref)
+    n = len(chunks)
     cols = [pl.ds(a * G, (b - a) * G) for a, b in chunks]
 
     def peer(d):
@@ -87,10 +156,9 @@
         blk = g_ref.at[p, st, x]
         return remote(blk, blk, ago_s.at[p, st, d - 1], ago_r.at[p, st, d - 1], xdev(d))
 
-    def own(st):
-        return remote(
-            b2_ref.at[st], g_ref.at[1, st, x], own_s.at[st], own_r.at[st],
-            (s + step_of[st], e),
+    def change(st):
+        return remote(
+            dl_ref.at[st], dr_ref.at[st], own_s.at[st], own_r.at[st], (s + step_of[st], e)
         )
 
     def rs1(p, st, d, c):
@@ -111,12 +179,17 @@
             rsz_s.at[p, st, c], rsz_r.at[p, st, c], zdev,
         )
 
-    def mid(st):
-        return remote(m1_ref.at[st], m2_ref.at[st], m_s.at[st], m_r.at[st], (s + step_of[st], e))
+    def shift(st):
+        return remote(x_ref.at[st], m2_ref.at[st], m_s.at[st], m_r.at[st], (s + step_of[st], e))
 
     def nslots(st):
         return remote(
-            mys_ref.at[st], nbs_ref.at[st], n_s.at[st], n_r.at[st], (s - step_of[st], e)
+            mys_ref.at[1, st], nbs_ref.at[st], n_s.at[st], n_r.at[st], (s - step_of[st], e)
+        )
+
+    def oslots(st):
+        return remote(
+            mys_ref.at[0, st], prs_ref.at[st], o_s.at[st], o_r.at[st], (s + step_of[st], e)
         )
 
     def place(k, q_row, rows):
@@ -144,12 +217,12 @@
 
     def first(st):
         def load(k):
-            return in_refs[st][0, :, pl.ds(k * G, G)].astype(F32)
+            return x_ref[st, :, pl.ds(k * G, G)].astype(F32)
 
         scale, affinity = stats(load)
         aff_ref[0, st] = jnp.broadcast_to(affinity, (tokens, 128))
         pack(
-            slot_refs[st][0, 0], lambda k: (load(k) * scale).astype(BF16), g_ref.at[0, st, x]
+            slots_ref[st, 0], lambda k: (load(k) * scale).astype(BF16), g_ref.at[0, st, x]
         )
 
     def gate_up(p, st):
@@ -191,10 +264,14 @@
         zs_ref[p, st, :, cols[c]] = total.astype(BF16)
         rsz(p, st, c).start()
 
+    def column(q_row):
+        eye = iota((tokens, tokens), 0) == iota((tokens, tokens), 1)
+        return jnp.sum(jnp.where(eye, q_row.astype(F32), 0.0), axis=1, keepdims=True)
+
     def finish(p, st, load, store):
         for d in (1, 2, 3):
             rs0(p, st, d).wait_recv()
-        for c in range(len(chunks)):
+        for c in range(n):
             rsz(p, st, c).wait_recv()
 
         def total(k):
@@ -205,9 +282,7 @@
             high = v.astype(BF16)
             return high, (v - high.astype(F32)).astype(BF16)
 
-        q_row = slot_refs[st][0, p].astype(F32)
-        eye = iota((tokens, tokens), 0) == iota((tokens, tokens), 1)
-        q_col = jnp.sum(jnp.where(eye, q_row, 0.0), axis=1, keepdims=True)
+        q_col = column(slots_ref[st, p])
         affinity = aff_ref[p, st, :, 0:1]
         tail_high, tail_low = total(groups)
         for k in range(groups):
@@ -219,21 +294,28 @@
 
     def finish_first(st):
         squares = [jnp.zeros((tokens, G), F32)]
+        tail = [jnp.zeros((MAIN, G), F32)]
 
         def load(k):
-            return in_refs[st][0, :, pl.ds(k * G, G)].astype(F32)
+            return x_ref[st, :, pl.ds(k * G, G)].astype(F32)
 
         def store(k, value):
             m1_ref[st, :, pl.ds(k * G, G)] = value
+            placed = place(k, slots_ref[st, 0], value)
+            dl_ref[st, :, pl.ds(k * G, G)] = placed[:MAIN].astype(BF16)
+            tail[0] = tail[0] + placed[MAIN:]
             value = value.astype(F32)
             squares[0] = squares[0] + value * value
 
         finish(0, st, load, store)
-        scale = lax.rsqrt(jnp.sum(squares[0], axis=1, keepdims=True) / width + EPS)
+        dl_ref[st, :, pl.ds(groups * G, G)] = tail[0].astype(BF16)
 
         @pl.when(has_next[st])
         def _():
+            change(st).start()
             nslots(st).wait_recv()
+
+        scale = lax.rsqrt(jnp.sum(squares[0], axis=1, keepdims=True) / width + EPS)
 
         def normed(k):
             return (m1_ref[st, :, pl.ds(k * G, G)].astype(F32) * scale).astype(BF16)
@@ -242,18 +324,41 @@
 
         @pl.when(has_next[st])
         def _():
-            for c in range(len(chunks)):
+            for c in range(n):
                 agz(1, st, c).start()
-            own(st).start()
-            mid(st).start()
+
+    def send_shift(st):
+        pl.when(has_next[st])(lambda: shift(st).start())
 
     def arrive_own(st):
         @pl.when(has_prev[st])
         def _():
-            own(st).wait_recv()
-
+            shift(st).wait_recv()
+            oslots(st).wait_recv()
+            change(st).wait_recv()
+
+        q_col = column(prs_ref[st, 0:1, 0:tokens])
+        kept = q_col >= float(CAP)
+        tail = dr_ref[st, :, pl.ds(groups * G, G)]
+        for k in range(groups):
+            where = pl.ds(k * G, G)
+            lane = iota((tokens, 2 * MAIN), 1)
+            pick = (q_col == slot_of_row(lane, k).astype(F32)).astype(F32).astype(BF16)
+            rows = dot(pick, jnp.concatenate([dr_ref[st, :, where], tail], axis=0))
+            rows = jnp.where(kept, m2_ref[st, :, where].astype(F32), rows)
+            m2_ref[st, :, where] = rows.astype(BF16)
+
+        def load(k):
+            return m2_ref[st, :, pl.ds(k * G, G)].astype(F32)
+
+        scale, affinity = stats(load)
+        aff_ref[1, st] = jnp.broadcast_to(affinity, (tokens, 128))
+        pack(slots_ref[st, 1], lambda k: (load(k) * scale).astype(BF16), g_ref.at[1, st, x])
+        send_own(1, st)
+
+    def send_own(p, st):
         for d in (2, 1, 3):
-            ago(1, st, d).start()
+            ago(p, st, d).start()
 
     def relay(p, st, c):
         if p == 0:
@@ -268,16 +373,8 @@
     def gathered(p, st):
         for d in (1, 2, 3):
             ago(p, st, d).wait_recv()
-            for c in range(len(chunks)):
+            for c in range(n):
                 agx(p, st, d, c).wait_recv()
-
-    def middle(st):
-        @pl.when(has_prev[st])
-        def _():
-            mid(st).wait_recv()
-
-        _, affinity = stats(lambda k: m2_ref[st, :, pl.ds(k * G, G)].astype(F32))
-        aff_ref[1, st] = jnp.broadcast_to(affinity, (tokens, 128))
 
     def finish_second(st):
         def load(k):
@@ -290,11 +387,11 @@
 
     def sent_gather(p, st):
         def late():
-            for c in range(len(chunks)):
+            for c in range(n):
                 agz(p, st, c).wait_send()
             if p == 1:
-                own(st).wait_send()
-                mid(st).wait_send()
+                change(st).wait_send()
+                shift(st).wait_send()
 
         if p == 0:
             late()
@@ -302,25 +399,16 @@
             pl.when(has_next[st])(late)
         for d in (1, 2, 3):
             ago(p, st, d).wait_send()
-            for c in range(len(chunks)):
+            for c in range(n):
                 agx(p, st, d, c).wait_send()
 
     def sent_reduce(p, st):
         for d in (1, 2, 3):
             rs0(p, st, d).wait_send()
-            for c in range(len(chunks)):
+            for c in range(n):
                 rs1(p, st, d, c).wait_send()
-        for c in range(len(chunks)):
+        for c in range(n):
             rsz(p, st, c).wait_send()
-
-    half = wg_hbm.shape[2]
-    weights = [
-        pltpu.make_async_copy(wg_hbm.at[0], wgu_ref.at[:, pl.ds(0, half)], w_sem.at[0]),
-        pltpu.make_async_copy(wu_hbm.at[0], wgu_ref.at[:, pl.ds(half, half)], w_sem.at[1]),
-        pltpu.make_async_copy(wd_hbm.at[0], wd_ref, w_sem.at[2]),
-    ]
-    for w in weights:
-        w.start()
 
     barrier = pltpu.get_barrier_semaphore()
 
@@ -336,10 +424,29 @@
             greet((s + step, e))
             greet((s + step, other))
 
+    half = wg_hbm.shape[2]
+    weights = [
+        pltpu.make_async_copy(wg_hbm.at[0], wgu_ref.at[:, pl.ds(0, half)], w_sem.at[0]),
+        pltpu.make_async_copy(wu_hbm.at[0], wgu_ref.at[:, pl.ds(half, half)], w_sem.at[1]),
+        pltpu.make_async_copy(wd_hbm.at[0], wd_ref, w_sem.at[2]),
+    ]
+    loads = [
+        pltpu.make_async_copy(up_hbm.at[0], x_ref.at[0], w_sem.at[3]),
+        pltpu.make_async_copy(router_hbm, router_ref, w_sem.at[4]),
+        pltpu.make_async_copy(su_hbm.at[0], slots_ref.at[0], w_sem.at[5]),
+        pltpu.make_async_copy(sd_hbm.at[0], slots_ref.at[1], w_sem.at[6]),
+        pltpu.make_async_copy(dn_hbm.at[0], x_ref.at[1], w_sem.at[7]),
+    ]
+    for copy in loads + weights:
+        copy.start()
+
+    for copy in loads[:4]:
+        copy.wait()
     first(0)
     for st in (0, 1):
-        mys_ref[st] = jnp.zeros(mys_ref.shape[1:], jnp.int32)
-        mys_ref[st, 0:1, 0:tokens] = slot_refs[st][0, 1]
+        for p in (0, 1):
+            mys_ref[p, st] = jnp.zeros(mys_ref.shape[2:], jnp.int32)
+            mys_ref[p, st, 0:1, 0:tokens] = slots_ref[st, p]
 
         @pl.when(jnp.logical_not(has_next[st]))
         def _(st=st):
@@ -347,84 +454,66 @@
 
         @pl.when(jnp.logical_not(has_prev[st]))
         def _(st=st):
-            g_ref[1, st, x] = jnp.zeros(g_ref.shape[3:], BF16)
+            prs_ref[st] = jnp.zeros(prs_ref.shape[1:], jnp.int32)
+            dr_ref[st] = jnp.zeros(dr_ref.shape[1:], BF16)
             g_ref[1, st, 4 + x] = jnp.zeros(g_ref.shape[3:], BF16)
             m2_ref[st] = jnp.zeros(m2_ref.shape[1:], BF16)
 
     neighbours = 4 + 2 * (s > 0).astype(jnp.int32) + 2 * (s < sections - 1).astype(jnp.int32)
     pl.semaphore_wait(barrier, neighbours)
 
-    def send_first(st):
-        for c in range(len(chunks)):
+    def begin(st):
+        if st == 1:
+            loads[4].wait()
+            first(1)
+        for c in range(n):
             agz(0, st, c).start()
-        for d in (2, 1, 3):
-            ago(0, st, d).start()
-
-    send_first(0)
-    first(1)
-    send_first(1)
-    for st in (0, 1):
-        @pl.when(has_prev[st])
-        def _(st=st):
-            nslots(st).start()
-
-    n = len(chunks)
-    for p in (0, 1):
-        for c in range(n):
-            relay(p, 0, c)
-        if p == 0:
-            for w in weights:
-                w.wait()
-        gathered(p, 0)
-        hidden = gate_up(p, 0)
+
+    def slots():
+        for st in (0, 1):
+            @pl.when(has_prev[st])
+            def _(st=st):
+                nslots(st).start()
+
+            @pl.when(has_next[st])
+            def _(st=st):
+                oslots(st).start()
+
+    def slots_sent():
+        for st in (0, 1):
+            pl.when(has_prev[st])(lambda st=st: nslots(st).wait_send())
+            pl.when(has_next[st])(lambda st=st: oslots(st).wait_send())
+
+    def weights_here():
+        for w in weights:
+            w.wait()
+
+    def compute(p, st):
+        gathered(p, st)
+        hidden = gate_up(p, st)
         tails = []
         for c in range(n):
-            down(p, 0, hidden, tails, c)
+            down(p, st, hidden, tails, c)
+
+    def send_rows(p, st):
         for d in (2, 1, 3):
-            rs0(p, 0, d).start()
-        if p == 1:
-            arrive_own(1)
-        relay(p, 1, 0)
-        relay(p, 1, 1)
-        reduce_other(p, 0, 0)
-        reduce_other(p, 0, 1)
-        relay(p, 1, 2)
-        reduce_other(p, 0, 2)
-        relay(p, 1, 3)
-        reduce_other(p, 0, 3)
-        gathered(p, 1)
-        hidden = gate_up(p, 1)
-        tails = []
-        for c in range(n):
-            down(p, 1, hidden, tails, c)
-        for d in (2, 1, 3):
-            rs0(p, 1, d).start()
-        for c in range(n):
-            reduce_other(p, 1, c)
-        if p == 0:
-            finish_first(0)
-            for st in (0, 1):
-                sent_gather(0, st)
-                sent_reduce(0, st)
-                pl.when(has_prev[st])(lambda st=st: nslots(st).wait_send())
-            finish_first(1)
-            arrive_own(0)
-            middle(0)
-        else:
-            middle(1)
-            for st in (0, 1):
-                sent_gather(1, st)
-            finish_second(0)
-            sent_reduce(1, 0)
-            finish_second(1)
-            sent_reduce(1, 1)
+            rs0(p, st, d).start()
+
+    steps = dict(
+        begin=begin, send_own=send_own, slots=slots, slots_sent=slots_sent, weights=weights_here,
+        relay=relay, own=arrive_own, compute=compute, send_rows=send_rows, reduce=reduce_other,
+        finish_first=finish_first, send_shift=send_shift,
+        finish_second=finish_second, sent_gather=sent_gather, sent_reduce=sent_reduce,
+    )
+    for name, *args in ORDER:
+        steps[name](*args)
 
 
 def shards(up_in, down_in, router, w_gate, w_up, w_down, slots_up, slots_down, *, sections):
     _, tokens, width = up_in.shape
     groups = width // G
     packed = width + G
-    ends = [(groups + 1) * i // 4 for i in range(5)]
+    ends = [(groups + 1) * i // CHUNKS for i in range(CHUNKS + 1)]
     chunks = list(zip(ends[:-1], ends[1:]))
     n = len(chunks)
     ffd = w_gate.shape[2]
@@ -436,9 +525,12 @@
         functools.partial(kernel_entry, chunks=chunks, sections=sections),
         name="relay_layers",
         out_shape=(out, out),
-        in_specs=[vmem] * 5 + [hbm] * 3,
+        in_specs=[hbm] * 8,
         out_specs=(vmem, vmem),
         scratch_shapes=[
+            pltpu.VMEM((2, tokens, width), BF16),
+            pltpu.VMEM((1, width), F32),
+            pltpu.VMEM((2, 2, 1, tokens), jnp.int32),
             pltpu.VMEM((2, 2, 8, MAIN, packed), BF16),
             pltpu.VMEM((2, 2, 8, MAIN, packed), BF16),
             pltpu.VMEM((2, 2, 3, MAIN, packed), BF16),
@@ -448,12 +540,15 @@
             pltpu.VMEM((2, MAIN, packed), BF16),
             pltpu.VMEM((2, tokens, width), BF16),
             pltpu.VMEM((2, tokens, width), BF16),
+            pltpu.VMEM((2, MAIN, packed), BF16),
+            pltpu.VMEM((2, MAIN, packed), BF16),
             pltpu.VMEM((2, 2, tokens, 128), F32),
+            pltpu.VMEM((2, 2, 8, 128), jnp.int32),
             pltpu.VMEM((2, 8, 128), jnp.int32),
             pltpu.VMEM((2, 8, 128), jnp.int32),
             pltpu.VMEM((width, 2 * ffd), BF16),
             pltpu.VMEM((ffd, width), BF16),
-            dma((3,)),
+            dma((8,)),
             dma((2, 2, n)), dma((2, 2, n)),
             dma((2, 2, 3, n)), dma((2, 2, 3, n)),
             dma((2, 2, 3)), dma((2, 2, 3)),
@@ -463,15 +558,16 @@
             dma((2, 2, n)), dma((2, 2, n)),
             dma((2,)), dma((2,)),
             dma((2,)), dma((2,)),
+            dma((2,)), dma((2,)),
         ],
         compiler_params=pltpu.CompilerParams(
-            collective_id=0, has_side_effects=True, vmem_limit_bytes=48 * 1024 * 1024
+            collective_id=0, has_side_effects=True, vmem_limit_bytes=VMEM_LIMIT
         ),
     )(up_in, down_in, router, slots_up, slots_down, w_gate, w_up, w_down)
 
 
 def kernel_entry(*refs, chunks, sections):
-    kernel(*refs[:24], chunks, sections, *refs[24:])
+    kernel(*refs[:30], chunks, sections, *refs[30:])
 
 
 def solution(mesh):

time: 160 us -> 146 us (0.912)
  the two profiles are of different devices: /device:TPU:8 before, /device:TPU:40 now
where the time goes in v2:
time: 146 us
  Pallas kernels  143 us (98%)
  local copies, waits for them, and re-layouts  2.64 us (2%)
    pallas_call x1, Pallas kernels, shards(): pl.pallas_call(functools.partial(kernel_entry, chunks=chunks, sections=se...  143 us

profile of v2, /device:TPU:40, one launch (start us, length us, event | category | flops | bytes accessed | tf_op | source)
XLA Modules:
  0.0 146.2 jit_solution(16014399019851549263)
XLA Ops:
  0.6 142.9 %relay_layers.1 = (bf16[1,64,3584]{2,1,0:T(8,128)(2,1)}, bf16[1,64,3584]{2,1,0:T(8,128)(2,1)}) custom-call(bf16[1,64,3584]{2,1,0:T(8,128)(2,1)} %refs_0_.1, bf16[1,64,3584]{2,1,0:T(8,128)(2,1)} %refs_1_.1, f32[1,3584]{1,0:T(1,128)} %refs_2_.1, s32[1,2,1,64]{3,2,1,0:T(1,128)} %refs_3_.1, s32[1,2,1,64]{3,2,1,0:T(1,128)} %refs_4_.1, ...), custom_call_target="tpu_custom_call" | custom-call | tf_op jit(solution)/shard_map/relay_layers/pallas_call | solution.py:524
  143.5 0.0 copy-start
  143.5 1.9 %copy.12 = bf16[1,64,3584]{2,1,0:T(8,128)(2,1)} copy(bf16[1,64,3584]{2,1,0:T(8,128)(2,1)} %get-tuple-element.4) | data formatting | bytes 917504
  145.4 0.0 copy-done
  145.4 0.8 copy.13
Async XLA Ops:
  143.5 1.9 %copy-start = (bf16[1,64,3584]{2,1,0:T(8,128)(2,1)S(1)}, bf16[1,64,3584]{2,1,0:T(8,128)(2,1)}, u32[]{:S(2)}) copy-start(bf16[1,64,3584]{2,1,0:T(8,128)(2,1)} %get-tuple-element.5) | copy-start | bytes 1376260

commit v3 on v2

--- a/solution.py
+++ b/solution.py
@@ -17,65 +17,58 @@
 
 
 VMEM_LIMIT = 62 * 1024 * 1024
-CHUNKS = 4
+CHUNKS = 2
+KEPT = 48
 ORDER = [
     ("begin", 0),
     ("send_own", 0, 0),
     ("begin", 1),
     ("slots",),
+    ("send_shift", 1),
+    ("relay_own", 0, 0),
+    ("send_shift", 0),
     ("send_own", 0, 1),
-    ("send_shift", 0),
-    ("send_shift", 1),
     ("relay", 0, 0, 0),
+    ("relay_own", 0, 1),
     ("relay", 0, 0, 1),
-    ("relay", 0, 0, 2),
-    ("relay", 0, 0, 3),
+    ("relay", 0, 1, 0),
     ("weights",),
-    ("relay", 0, 1, 0),
     ("compute", 0, 0),
     ("relay", 0, 1, 1),
     ("reduce", 0, 0, 0),
-    ("relay", 0, 1, 3),
     ("reduce", 0, 0, 1),
-    ("relay", 0, 1, 2),
-    ("reduce", 0, 0, 3),
     ("send_rows", 0, 0),
-    ("reduce", 0, 0, 2),
     ("compute", 0, 1),
     ("send_rows", 0, 1),
+    ("reduce", 0, 1, 0),
     ("reduce", 0, 1, 1),
-    ("reduce", 0, 1, 2),
-    ("reduce", 0, 1, 3),
-    ("reduce", 0, 1, 0),
+    ("pass_rows", 0, 0),
+    ("pass_rows", 0, 1),
     ("finish_first", 0),
+    ("finish_first", 1),
     ("own", 0),
-    ("finish_first", 1),
+    ("relay_own", 1, 0),
     ("relay", 1, 0, 0),
     ("relay", 1, 0, 1),
-    ("relay", 1, 0, 2),
     ("own", 1),
-    ("relay", 1, 0, 3),
+    ("compute", 1, 0),
     ("relay", 1, 1, 0),
+    ("reduce", 1, 0, 1),
+    ("reduce", 1, 0, 0),
     ("relay", 1, 1, 1),
-    ("compute", 1, 0),
-    ("reduce", 1, 0, 0),
-    ("relay", 1, 1, 3),
-    ("reduce", 1, 0, 2),
-    ("reduce", 1, 0, 1),
-    ("relay", 1, 1, 2),
+    ("relay_own", 1, 1),
     ("compute", 1, 1),
     ("slots_sent",),
     ("sent_gather", 0, 0),
     ("sent_gather", 0, 1),
     ("send_rows", 1, 1),
-    ("reduce", 1, 0, 3),
     ("reduce", 1, 1, 0),
     ("reduce", 1, 1, 1),
-    ("reduce", 1, 1, 2),
-    ("reduce", 1, 1, 3),
     ("send_rows", 1, 0),
     ("sent_reduce", 0, 0),
     ("sent_reduce", 0, 1),
+    ("pass_rows", 1, 1),
+    ("pass_rows", 1, 0),
     ("sent_gather", 1, 0),
     ("sent_gather", 1, 1),
     ("finish_second", 0),
@@ -104,10 +97,10 @@
     up_hbm, dn_hbm, router_hbm, su_hbm, sd_hbm, wg_hbm, wu_hbm, wd_hbm,
     uo_ref, do_ref,
     x_ref, router_ref, slots_ref,
-    g_ref, p_ref, r0_ref, r1_ref, zs_ref, zr_ref, b2_ref, m1_ref, m2_ref, dl_ref, dr_ref,
+    g_ref, p_ref, ra_ref, sb_ref, rb_ref, rd_ref, r1_ref, xs_ref, xr_ref, zs_ref, zr_ref, b2_ref, m1_ref, m2_ref, dl_ref, dr_ref,
     aff_ref, mys_ref, nbs_ref, prs_ref, wgu_ref, wd_ref, chunks, sections,
-    w_sem, agz_s, agz_r, agx_s, agx_r, ago_s, ago_r, own_s, own_r,
-    rs1_s, rs1_r, rs0_s, rs0_r, rsz_s, rsz_r, m_s, m_r, n_s, n_r, o_s, o_r,
+    w_sem, agz_s, agz_r, agx_s, agx_r, ago_s, ago_r, agp_s, agp_r, own_s, own_r,
+    rs1_s, rs1_r, rsa_s, rsa_r, rsb_s, rsb_r, rsd_s, rsd_r, rsz_s, rsz_r, m_s, m_r, n_s, n_r, o_s, o_r,
 ):
     s = lax.axis_index("section")
     e = lax.axis_index("expert")
@@ -121,8 +114,13 @@
     n = len(chunks)
     cols = [pl.ds(a * G, (b - a) * G) for a, b in chunks]
 
+    pieces = [pl.ds(0, groups // 2 * G), pl.ds(groups // 2 * G, (groups + 1 - groups // 2) * G)]
+
     def peer(d):
-        return lax.rem(x + d, 4)
+        return lax.rem(x + d % 4, 4)
+
+    def way(c):
+        return 1 if c == 0 else -1
 
     def xdev(d):
         return (s, peer(d) * 2 + h)
@@ -152,9 +150,14 @@
         blk = g_ref.at[p, st, 4 + x, :, cols[c]]
         return remote(blk, blk, agx_s.at[p, st, d - 1, c], agx_r.at[p, st, d - 1, c], xdev(d))
 
-    def ago(p, st, d):
-        blk = g_ref.at[p, st, x]
-        return remote(blk, blk, ago_s.at[p, st, d - 1], ago_r.at[p, st, d - 1], xdev(d))
+    def ago(p, st, d, c):
+        blk = g_ref.at[p, st, x, :, pieces[c]]
+        i = (d + 1) // 2
+        return remote(blk, blk, ago_s.at[p, st, i, c], ago_r.at[p, st, i, c], xdev(d))
+
+    def agp(p, st, c):
+        blk = g_ref.at[p, st, peer(-way(c)), :, pieces[c]]
+        return remote(blk, blk, agp_s.at[p, st, c], agp_r.at[p, st, c], xdev(way(c)))
 
     def change(st):
         return remote(
@@ -167,10 +170,22 @@
             rs1_s.at[p, st, d - 1, c], rs1_r.at[p, st, d - 1, c], xdev(d),
         )
 
-    def rs0(p, st, d):
-        return remote(
-            p_ref.at[p, st, peer(d)], r0_ref.at[p, st, d - 1],
-            rs0_s.at[p, st, d - 1], rs0_r.at[p, st, d - 1], xdev(d),
+    def rsa(p, st, c):
+        return remote(
+            p_ref.at[p, st, peer(2), :, pieces[c]], ra_ref.at[p, st, :, pieces[c]],
+            rsa_s.at[p, st, c], rsa_r.at[p, st, c], xdev(way(c)),
+        )
+
+    def rsb(p, st, c):
+        return remote(
+            sb_ref.at[p, st, :, pieces[c]], rb_ref.at[p, st, :, pieces[c]],
+            rsb_s.at[p, st, c], rsb_r.at[p, st, c], xdev(way(c)),
+        )
+
+    def rsd(p, st, c):
+        return remote(
+            p_ref.at[p, st, peer(-way(c)), :, pieces[c]], rd_ref.at[p, st, :, pieces[c]],
+            rsd_s.at[p, st, c], rsd_r.at[p, st, c], xdev(-way(c)),
         )
 
     def rsz(p, st, c):
@@ -180,7 +195,9 @@
         )
 
     def shift(st):
-        return remote(x_ref.at[st], m2_ref.at[st], m_s.at[st], m_r.at[st], (s + step_of[st], e))
+        return remote(
+            xs_ref.at[st], xr_ref.at[st], m_s.at[st], m_r.at[st], (s + step_of[st], e)
+        )
 
     def nslots(st):
         return remote(
@@ -269,16 +286,16 @@
         return jnp.sum(jnp.where(eye, q_row.astype(F32), 0.0), axis=1, keepdims=True)
 
     def finish(p, st, load, store):
-        for d in (1, 2, 3):
-            rs0(p, st, d).wait_recv()
+        for c in (0, 1):
+            rsd(p, st, c).wait_recv()
+            rsb(p, st, c).wait_recv()
         for c in range(n):
             rsz(p, st, c).wait_recv()
 
         def total(k):
             at = pl.ds(k * G, G)
             v = p_ref[p, st, x, :, at].astype(F32) + zr_ref[p, st, :, at].astype(F32)
-            for d in (1, 2, 3):
-                v = v + r0_ref[p, st, d - 1, :, at].astype(F32)
+            v = v + rb_ref[p, st, :, at].astype(F32) + rd_ref[p, st, :, at].astype(F32)
             high = v.astype(BF16)
             return high, (v - high.astype(F32)).astype(BF16)
 
@@ -328,6 +345,10 @@
                 agz(1, st, c).start()
 
     def send_shift(st):
+        pick = (slots_ref[st, 0] == iota((KEPT, tokens), 0) + CAP).astype(F32).astype(BF16)
+        for k in range(groups):
+            where = pl.ds(k * G, G)
+            xs_ref[st, :, where] = dot(pick, x_ref[st, :, where]).astype(BF16)
         pl.when(has_next[st])(lambda: shift(st).start())
 
     def arrive_own(st):
@@ -338,15 +359,15 @@
             change(st).wait_recv()
 
         q_col = column(prs_ref[st, 0:1, 0:tokens])
-        kept = q_col >= float(CAP)
+        lane = iota((tokens, KEPT), 1) + CAP
+        kept = (q_col == lane.astype(F32)).astype(F32).astype(BF16)
         tail = dr_ref[st, :, pl.ds(groups * G, G)]
         for k in range(groups):
             where = pl.ds(k * G, G)
             lane = iota((tokens, 2 * MAIN), 1)
             pick = (q_col == slot_of_row(lane, k).astype(F32)).astype(F32).astype(BF16)
             rows = dot(pick, jnp.concatenate([dr_ref[st, :, where], tail], axis=0))
-            rows = jnp.where(kept, m2_ref[st, :, where].astype(F32), rows)
-            m2_ref[st, :, where] = rows.astype(BF16)
+            m2_ref[st, :, where] = (rows + dot(kept, xr_ref[st, :, where])).astype(BF16)
 
         def load(k):
             return m2_ref[st, :, pl.ds(k * G, G)].astype(F32)
@@ -357,8 +378,14 @@
         send_own(1, st)
 
     def send_own(p, st):
-        for d in (2, 1, 3):
-            ago(p, st, d).start()
+        for c in (0, 1):
+            for d in (way(c), -way(c)):
+                ago(p, st, d, c).start()
+
+    def relay_own(p, st):
+        for c in (0, 1):
+            ago(p, st, way(c), c).wait_recv()
+            agp(p, st, c).start()
 
     def relay(p, st, c):
         if p == 0:
@@ -371,8 +398,10 @@
             agx(p, st, d, c).start()
 
     def gathered(p, st):
+        for c in (0, 1):
+            ago(p, st, -way(c), c).wait_recv()
+            agp(p, st, c).wait_recv()
         for d in (1, 2, 3):
-            ago(p, st, d).wait_recv()
             for c in range(n):
                 agx(p, st, d, c).wait_recv()
 
@@ -397,14 +426,20 @@
             late()
         else:
             pl.when(has_next[st])(late)
+        for c in (0, 1):
+            agp(p, st, c).wait_send()
+            for d in (1, -1):
+                ago(p, st, d, c).wait_send()
         for d in (1, 2, 3):
-            ago(p, st, d).wait_send()
             for c in range(n):
                 agx(p, st, d, c).wait_send()
 
     def sent_reduce(p, st):
+        for c in (0, 1):
+            rsa(p, st, c).wait_send()
+            rsb(p, st, c).wait_send()
+            rsd(p, st, c).wait_send()
         for d in (1, 2, 3):
-            rs0(p, st, d).wait_send()
             for c in range(n):
                 rs1(p, st, d, c).wait_send()
         for c in range(n):
@@ -457,7 +492,7 @@
             prs_ref[st] = jnp.zeros(prs_ref.shape[1:], jnp.int32)
             dr_ref[st] = jnp.zeros(dr_ref.shape[1:], BF16)
             g_ref[1, st, 4 + x] = jnp.zeros(g_ref.shape[3:], BF16)
-            m2_ref[st] = jnp.zeros(m2_ref.shape[1:], BF16)
+            xr_ref[st] = jnp.zeros(xr_ref.shape[1:], BF16)
 
     neighbours = 4 + 2 * (s > 0).astype(jnp.int32) + 2 * (s < sections - 1).astype(jnp.int32)
     pl.semaphore_wait(barrier, neighbours)
@@ -496,12 +531,21 @@
             down(p, st, hidden, tails, c)
 
     def send_rows(p, st):
-        for d in (2, 1, 3):
-            rs0(p, st, d).start()
+        for c in (0, 1):
+            rsa(p, st, c).start()
+            rsd(p, st, c).start()
+
+    def pass_rows(p, st):
+        for c in (0, 1):
+            rsa(p, st, c).wait_recv()
+            total = p_ref[p, st, peer(way(c)), :, pieces[c]].astype(F32)
+            total = total + ra_ref[p, st, :, pieces[c]].astype(F32)
+            sb_ref[p, st, :, pieces[c]] = total.astype(BF16)
+            rsb(p, st, c).start()
 
     steps = dict(
         begin=begin, send_own=send_own, slots=slots, slots_sent=slots_sent, weights=weights_here,
-        relay=relay, own=arrive_own, compute=compute, send_rows=send_rows, reduce=reduce_other,
+        relay=relay, own=arrive_own, compute=compute, send_rows=send_rows, pass_rows=pass_rows, relay_own=relay_own, reduce=reduce_other,
         finish_first=finish_first, send_shift=send_shift,
         finish_second=finish_second, sent_gather=sent_gather, sent_reduce=sent_reduce,
     )
@@ -533,8 +577,13 @@
             pltpu.VMEM((2, 2, 1, tokens), jnp.int32),
             pltpu.VMEM((2, 2, 8, MAIN, packed), BF16),
             pltpu.VMEM((2, 2, 8, MAIN, packed), BF16),
+            pltpu.VMEM((2, 2, MAIN, packed), BF16),
+            pltpu.VMEM((2, 2, MAIN, packed), BF16),
+            pltpu.VMEM((2, 2, MAIN, packed), BF16),
+            pltpu.VMEM((2, 2, MAIN, packed), BF16),
             pltpu.VMEM((2, 2, 3, MAIN, packed), BF16),
-            pltpu.VMEM((2, 2, 3, MAIN, packed), BF16),
+            pltpu.VMEM((2, KEPT, width), BF16),
+            pltpu.VMEM((2, KEPT, width), BF16),
             pltpu.VMEM((2, 2, MAIN, packed), BF16),
             pltpu.VMEM((2, 2, MAIN, packed), BF16),
             pltpu.VMEM((2, MAIN, packed), BF16),
@@ -551,10 +600,13 @@
             dma((8,)),
             dma((2, 2, n)), dma((2, 2, n)),
             dma((2, 2, 3, n)), dma((2, 2, 3, n)),
-            dma((2, 2, 3)), dma((2, 2, 3)),
+            dma((2, 2, 2, 2)), dma((2, 2, 2, 2)),
+            dma((2, 2, 2)), dma((2, 2, 2)),
             dma((2,)), dma((2,)),
             dma((2, 2, 3, n)), dma((2, 2, 3, n)),
-            dma((2, 2, 3)), dma((2, 2, 3)),
+            dma((2, 2, 2)), dma((2, 2, 2)),
+            dma((2, 2, 2)), dma((2, 2, 2)),
+            dma((2, 2, 2)), dma((2, 2, 2)),
             dma((2, 2, n)), dma((2, 2, n)),
             dma((2,)), dma((2,)),
             dma((2,)), dma((2,)),
@@ -567,7 +619,7 @@
 
 
 def kernel_entry(*refs, chunks, sections):
-    kernel(*refs[:30], chunks, sections, *refs[30:])
+    kernel(*refs[:35], chunks, sections, *refs[35:])
 
 
 def solution(mesh):

time: 146 us -> 148 us (1.014)
  the two profiles are of different devices: /device:TPU:40 before, /device:TPU:8 now
where the time goes in v3:
time: 148 us
  Pallas kernels  145 us (98%)
  local copies, waits for them, and re-layouts  2.64 us (2%)
    pallas_call x1, Pallas kernels, shards(): pl.pallas_call(functools.partial(kernel_entry, chunks=chunks, sections=se...  145 us

profile of v3, /device:TPU:8, one launch (start us, length us, event | category | flops | bytes accessed | tf_op | source)
XLA Modules:
  0.0 147.9 jit_solution(2938733394932581536)
XLA Ops:
  0.6 144.6 %relay_layers.1 = (bf16[1,64,3584]{2,1,0:T(8,128)(2,1)}, bf16[1,64,3584]{2,1,0:T(8,128)(2,1)}) custom-call(bf16[1,64,3584]{2,1,0:T(8,128)(2,1)} %refs_0_.1, bf16[1,64,3584]{2,1,0:T(8,128)(2,1)} %refs_1_.1, f32[1,3584]{1,0:T(1,128)} %refs_2_.1, s32[1,2,1,64]{3,2,1,0:T(1,128)} %refs_3_.1, s32[1,2,1,64]{3,2,1,0:T(1,128)} %refs_4_.1, ...), custom_call_target="tpu_custom_call" | custom-call | tf_op jit(solution)/shard_map/relay_layers/pallas_call | solution.py:568
  145.2 0.0 copy-start
  145.2 1.9 %copy.12 = bf16[1,64,3584]{2,1,0:T(8,128)(2,1)} copy(bf16[1,64,3584]{2,1,0:T(8,128)(2,1)} %get-tuple-element.4) | data formatting | bytes 917504
  147.1 0.0 copy-done
  147.1 0.8 copy.13
Async XLA Ops:
  145.2 1.9 %copy-start = (bf16[1,64,3584]{2,1,0:T(8,128)(2,1)S(1)}, bf16[1,64,3584]{2,1,0:T(8,128)(2,1)}, u32[]{:S(2)}) copy-start(bf16[1,64,3584]{2,1,0:T(8,128)(2,1)} %get-tuple-element.5) | copy-start | bytes 1376260

commit v4 on v3

--- a/solution.py
+++ b/solution.py
@@ -17,53 +17,69 @@
 
 
 VMEM_LIMIT = 62 * 1024 * 1024
-CHUNKS = 2
+CHUNKS = 4
 KEPT = 48
 ORDER = [
     ("begin", 0),
     ("send_own", 0, 0),
     ("begin", 1),
     ("slots",),
-    ("send_shift", 1),
-    ("relay_own", 0, 0),
+    ("relay", 0, 0, 0),
     ("send_shift", 0),
     ("send_own", 0, 1),
-    ("relay", 0, 0, 0),
-    ("relay_own", 0, 1),
+    ("send_shift", 1),
     ("relay", 0, 0, 1),
+    ("relay_own", 0, 0),
+    ("relay", 0, 0, 2),
+    ("relay", 0, 0, 3),
     ("relay", 0, 1, 0),
     ("weights",),
     ("compute", 0, 0),
     ("relay", 0, 1, 1),
+    ("reduce", 0, 0, 1),
+    ("relay", 0, 1, 3),
+    ("reduce", 0, 0, 2),
+    ("relay", 0, 1, 2),
+    ("reduce", 0, 0, 3),
+    ("relay_own", 0, 1),
     ("reduce", 0, 0, 0),
-    ("reduce", 0, 0, 1),
     ("send_rows", 0, 0),
     ("compute", 0, 1),
-    ("send_rows", 0, 1),
     ("reduce", 0, 1, 0),
     ("reduce", 0, 1, 1),
+    ("reduce", 0, 1, 3),
+    ("reduce", 0, 1, 2),
     ("pass_rows", 0, 0),
+    ("send_rows", 0, 1),
     ("pass_rows", 0, 1),
     ("finish_first", 0),
+    ("own", 0),
     ("finish_first", 1),
-    ("own", 0),
-    ("relay_own", 1, 0),
     ("relay", 1, 0, 0),
     ("relay", 1, 0, 1),
+    ("relay_own", 1, 0),
+    ("relay", 1, 0, 2),
+    ("relay", 1, 0, 3),
     ("own", 1),
+    ("relay", 1, 1, 0),
     ("compute", 1, 0),
-    ("relay", 1, 1, 0),
+    ("relay", 1, 1, 1),
+    ("relay", 1, 1, 2),
     ("reduce", 1, 0, 1),
+    ("relay", 1, 1, 3),
+    ("reduce", 1, 0, 2),
+    ("reduce", 1, 0, 3),
     ("reduce", 1, 0, 0),
-    ("relay", 1, 1, 1),
     ("relay_own", 1, 1),
     ("compute", 1, 1),
     ("slots_sent",),
     ("sent_gather", 0, 0),
     ("sent_gather", 0, 1),
+    ("reduce", 1, 1, 0),
     ("send_rows", 1, 1),
-    ("reduce", 1, 1, 0),
     ("reduce", 1, 1, 1),
+    ("reduce", 1, 1, 3),
+    ("reduce", 1, 1, 2),
     ("send_rows", 1, 0),
     ("sent_reduce", 0, 0),
     ("sent_reduce", 0, 1),
@@ -405,14 +421,18 @@
             for c in range(n):
                 agx(p, st, d, c).wait_recv()
 
+    def result(st):
+        return pltpu.make_async_copy(m2_ref.at[st], out_refs[st].at[0], w_sem.at[8 + st])
+
     def finish_second(st):
         def load(k):
             return m2_ref[st, :, pl.ds(k * G, G)].astype(F32)
 
         def store(k, value):
-            out_refs[st][0, :, pl.ds(k * G, G)] = value
+            m2_ref[st, :, pl.ds(k * G, G)] = value
 
         finish(1, st, load, store)
+        result(st).start()
 
     def sent_gather(p, st):
         def late():
@@ -551,6 +571,8 @@
     )
     for name, *args in ORDER:
         steps[name](*args)
+    for st in (0, 1):
+        result(st).wait()
 
 
 def shards(up_in, down_in, router, w_gate, w_up, w_down, slots_up, slots_down, *, sections):
@@ -561,7 +583,6 @@
     chunks = list(zip(ends[:-1], ends[1:]))
     n = len(chunks)
     ffd = w_gate.shape[2]
-    vmem = pl.BlockSpec(memory_space=pltpu.VMEM)
     hbm = pl.BlockSpec(memory_space=pl.ANY)
     dma = pltpu.SemaphoreType.DMA
     out = jax.ShapeDtypeStruct(up_in.shape, BF16)
@@ -570,7 +591,7 @@
         name="relay_layers",
         out_shape=(out, out),
         in_specs=[hbm] * 8,
-        out_specs=(vmem, vmem),
+        out_specs=(hbm, hbm),
         scratch_shapes=[
             pltpu.VMEM((2, tokens, width), BF16),
             pltpu.VMEM((1, width), F32),
@@ -597,7 +618,7 @@
             pltpu.VMEM((2, 8, 128), jnp.int32),
             pltpu.VMEM((width, 2 * ffd), BF16),
             pltpu.VMEM((ffd, width), BF16),
-            dma((8,)),
+            dma((10,)),
             dma((2, 2, n)), dma((2, 2, n)),
             dma((2, 2, 3, n)), dma((2, 2, 3, n)),
             dma((2, 2, 2, 2)), dma((2, 2, 2, 2)),

time: 148 us -> 145 us (0.980)
  the two profiles are of different devices: /device:TPU:8 before, /device:TPU:16 now
where the time goes in v4:
time: 145 us
  Pallas kernels  142 us (98%)
  local copies, waits for them, and re-layouts  2.64 us (2%)
    pallas_call x1, Pallas kernels, shards(): pl.pallas_call(functools.partial(kernel_entry, chunks=chunks, sections=se...  142 us

profile of v4, /device:TPU:16, one launch (start us, length us, event | category | flops | bytes accessed | tf_op | source)
XLA Modules:
  0.0 144.9 jit_solution(17286225101694302023)
XLA Ops:
  0.6 141.6 %relay_layers.1 = (bf16[1,64,3584]{2,1,0:T(8,128)(2,1)}, bf16[1,64,3584]{2,1,0:T(8,128)(2,1)}) custom-call(bf16[1,64,3584]{2,1,0:T(8,128)(2,1)} %refs_0_.1, bf16[1,64,3584]{2,1,0:T(8,128)(2,1)} %refs_1_.1, f32[1,3584]{1,0:T(1,128)} %refs_2_.1, s32[1,2,1,64]{3,2,1,0:T(1,128)} %refs_3_.1, s32[1,2,1,64]{3,2,1,0:T(1,128)} %refs_4_.1, ...), custom_call_target="tpu_custom_call" | custom-call | tf_op jit(solution)/shard_map/relay_layers/pallas_call | solution.py:589
  142.2 0.0 copy-start
  142.2 1.9 %copy.12 = bf16[1,64,3584]{2,1,0:T(8,128)(2,1)} copy(bf16[1,64,3584]{2,1,0:T(8,128)(2,1)} %get-tuple-element.4) | data formatting | bytes 917504
  144.1 0.0 copy-done
  144.1 0.8 copy.13
Async XLA Ops:
  142.2 1.9 %copy-start = (bf16[1,64,3584]{2,1,0:T(8,128)(2,1)S(1)}, bf16[1,64,3584]{2,1,0:T(8,128)(2,1)}, u32[]{:S(2)}) copy-start(bf16[1,64,3584]{2,1,0:T(8,128)(2,1)} %get-tuple-element.5) | copy-start | bytes 1376260

commit v5 on v4

--- a/solution.py
+++ b/solution.py
@@ -492,11 +492,13 @@
         pltpu.make_async_copy(sd_hbm.at[0], slots_ref.at[1], w_sem.at[6]),
         pltpu.make_async_copy(dn_hbm.at[0], x_ref.at[1], w_sem.at[7]),
     ]
-    for copy in loads + weights:
+    for copy in loads:
         copy.start()
 
     for copy in loads[:4]:
         copy.wait()
+    for copy in weights:
+        copy.start()
     first(0)
     for st in (0, 1):
         for p in (0, 1):

time: 145 us -> 145 us (level)
  no operation moved by 1% of the time
where the time goes in v5:
time: 145 us
  Pallas kernels  142 us (98%)
  local copies, waits for them, and re-layouts  2.64 us (2%)
    pallas_call x1, Pallas kernels, shards(): pl.pallas_call(functools.partial(kernel_entry, chunks=chunks, sections=se...  142 us

profile of v5, /device:TPU:16, one launch (start us, length us, event | category | flops | bytes accessed | tf_op | source)
XLA Modules:
  0.0 144.9 jit_solution(17921683443483995828)
XLA Ops:
  0.6 141.6 %relay_layers.1 = (bf16[1,64,3584]{2,1,0:T(8,128)(2,1)}, bf16[1,64,3584]{2,1,0:T(8,128)(2,1)}) custom-call(bf16[1,64,3584]{2,1,0:T(8,128)(2,1)} %refs_0_.1, bf16[1,64,3584]{2,1,0:T(8,128)(2,1)} %refs_1_.1, f32[1,3584]{1,0:T(1,128)} %refs_2_.1, s32[1,2,1,64]{3,2,1,0:T(1,128)} %refs_3_.1, s32[1,2,1,64]{3,2,1,0:T(1,128)} %refs_4_.1, ...), custom_call_target="tpu_custom_call" | custom-call | tf_op jit(solution)/shard_map/relay_layers/pallas_call | solution.py:591
  142.2 0.0 copy-start
  142.2 1.9 %copy.12 = bf16[1,64,3584]{2,1,0:T(8,128)(2,1)} copy(bf16[1,64,3584]{2,1,0:T(8,128)(2,1)} %get-tuple-element.4) | data formatting | bytes 917504
  144.1 0.0 copy-done
  144.1 0.8 copy.13
Async XLA Ops:
  142.2 1.9 %copy-start = (bf16[1,64,3584]{2,1,0:T(8,128)(2,1)S(1)}, bf16[1,64,3584]{2,1,0:T(8,128)(2,1)}, u32[]{:S(2)}) copy-start(bf16[1,64,3584]{2,1,0:T(8,128)(2,1)} %get-tuple-element.5) | copy-start | bytes 1376260
